TPU v7x, 256 devices: a whole 4x4x8 slice. The times are simulated.
256 devices in a mesh: row: 32 (over z, y_hi, core), col: 8 (over y_lo, x).
Axes of the slice: x: 4, y: 4 (y_hi: 2, y_lo: 2; y = y_hi * 2 + y_lo), z: 8, core: 2. Of those that a mesh axis runs over, the one named last changes fastest.
Arguments:
- features: bfloat16 [512, 512, 384], P('row', 'col'), may hold values from -30 to 30
- inner_weights: bfloat16 [4, 3, 3, 384, 384], replicated, may hold values from -0.109375 to 0.109375
- far_weights: bfloat16 [3, 3, 384, 384], replicated, may hold values from -0.109375 to 0.109375
- gains: float32 [5, 384], replicated, may hold values from 0.1 to 1.9
Outputs:
- result: float32 [512, 512, 384], P('row', 'col')
All inputs are finite; a program needn't handle non-finite values.
Results may differ from a plain program's by a relative error of at most 0.0024.
Values may be sent and summed in bfloat16 or wider, within the bound.
A program may use at most 192 MiB of HBM per device.

v0:
```python
import functools

import jax
import jax.numpy as jnp
from jax import lax
from jax.experimental import pallas as pl
from jax.experimental.pallas import tpu as pltpu
from jax.sharding import PartitionSpec as P

MESH = pl.DeviceIdType.MESH
CH = 384
HOP = 4
ROWS, COLS = 16, 64
WIDE = 80
R = 4


def norm_act(stream, gain, mask):
    centre = jnp.mean(stream, axis=-1, keepdims=True)
    moved = stream - centre
    spread = jnp.mean(moved * moved, axis=-1, keepdims=True)
    scale = lax.rsqrt(spread + 1e-05)
    if mask is not None:
        scale = scale * mask
    return jax.nn.gelu(moved * scale * gain).astype(jnp.bfloat16)


def dot(a, b):
    return jnp.dot(a, b, preferred_element_type=jnp.float32)


def loop(n, body):
    def step(i, carry):
        body(i)
        return carry

    lax.fori_loop(0, n, step, 0)


def kernel(
    nrow, ncol,
    feat, inner, far, gains, out,
    fx, hl, hr, u0, u1, u2, u3, s, w, wf,
    edge, edge_out, edge_in, fa, fr, fp, fq,
    in_sem, w_sem, o_sem,
    e0_s, e0_r, e2_s, e2_r, e3_s, e3_r, ed_s, ed_r, fa_s, fa_r, fp_s, fp_r,
):
    r, c = lax.axis_index("row"), lax.axis_index("col")

    def there(dr, dc):
        return (r + dr >= 0) & (r + dr < nrow) & (c + dc >= 0) & (c + dc < ncol)

    def remote(src, dst, ss, rs, dr, dc):
        return pltpu.make_async_remote_copy(
            src_ref=src, dst_ref=dst, send_sem=ss, recv_sem=rs,
            device_id=(r + dr, c + dc), device_id_type=MESH,
        )

    def send(src, dst, ss, rs, dr, dc):
        @pl.when(there(dr, dc))
        def _():
            remote(src, dst, ss, rs, dr, dc).start()

    def sent(src, dst, ss, rs, dr, dc):
        @pl.when(there(dr, dc))
        def _():
            remote(src, dst, ss, rs, dr, dc).wait_send()

    def received(dst, ss, rs, dr, dc):
        @pl.when(there(dr, dc))
        def _():
            remote(dst, dst, ss, rs, dr, dc).wait_recv()

    own_copy = pltpu.make_async_copy(feat, fx.at[pl.ds(3, ROWS), pl.ds(0, COLS)], in_sem)
    own_copy.start()

    def weights(l):
        for b in range(3):
            pltpu.make_async_copy(
                inner.at[l, :, b], w.at[l, :, :, pl.ds(b * CH, CH)], w_sem.at[l]
            ).start()

    weights(0)

    greet = [(dr, dc) for dr in (-1, 0, 1) for dc in (-1, 0, 1) if dr or dc] + [(HOP, 0), (-HOP, 0)]
    barrier = pltpu.get_barrier_semaphore()
    for dr, dc in greet:
        @pl.when(there(dr, dc))
        def _():
            pl.semaphore_signal(barrier, inc=1, device_id=(r + dr, c + dc), device_id_type=MESH)


    @pl.when(r == 0)
    def _():
        fx[0:3] = jnp.zeros((3, WIDE, CH), fx.dtype)
        hl[0:3] = jnp.zeros((3, 16, CH), hl.dtype)
        hr[0:3] = jnp.zeros((3, 16, CH), hr.dtype)
        u2[0:4] = jnp.zeros((4, WIDE, CH), u2.dtype)
        u3[0:8] = jnp.zeros((8, COLS, CH), u3.dtype)

    @pl.when(r == nrow - 1)
    def _():
        fx[19:22] = jnp.zeros((3, WIDE, CH), fx.dtype)
        hl[19:22] = jnp.zeros((3, 16, CH), hl.dtype)
        hr[19:22] = jnp.zeros((3, 16, CH), hr.dtype)
        u2[20:24] = jnp.zeros((4, WIDE, CH), u2.dtype)
        u3[24:32] = jnp.zeros((8, COLS, CH), u3.dtype)

    tile_zero = jnp.zeros((R, COLS, CH), jnp.bfloat16)

    @pl.when(c == 0)
    def _():
        hl[...] = jnp.zeros(hl.shape, hl.dtype)
        for k in range(4):
            edge_in[k, 0] = jnp.zeros((R * 8, CH), edge_in.dtype)
            (fr if k % 2 == 0 else fq)[k, 0] = tile_zero

    @pl.when(c == ncol - 1)
    def _():
        hr[...] = jnp.zeros(hr.shape, hr.dtype)
        for k in range(4):
            edge_in[k, 1] = jnp.zeros((R * 8, CH), edge_in.dtype)
            (fr if k % 2 == 0 else fq)[k, 1] = tile_zero

    @pl.when(r < HOP)
    def _():
        for k in range(4):
            (fr if k % 2 == 1 else fq)[k, 0] = tile_zero

    @pl.when(r >= nrow - HOP)
    def _():
        for k in range(4):
            (fr if k % 2 == 1 else fq)[k, 1] = tile_zero

    pl.semaphore_wait(barrier, sum(jnp.where(there(dr, dc), 1, 0) for dr, dc in greet))

    low, high, whole = pl.ds(0, 3), pl.ds(13, 3), pl.ds(0, ROWS)
    left16, right16 = pl.ds(0, 16), pl.ds(COLS - 16, 16)
    top, mid, bottom = pl.ds(0, 3), pl.ds(3, ROWS), pl.ds(19, 3)
    first = [
        (feat.at[low], fx.at[bottom, pl.ds(0, COLS)], -1, 0),
        (feat.at[high], fx.at[top, pl.ds(0, COLS)], 1, 0),
        (feat.at[low, left16], hr.at[bottom], -1, -1),
        (feat.at[low, right16], hl.at[bottom], -1, 1),
        (feat.at[high, left16], hr.at[top], 1, -1),
        (feat.at[high, right16], hl.at[top], 1, 1),
        (feat.at[whole, left16], hr.at[mid], 0, -1),
        (feat.at[whole, right16], hl.at[mid], 0, 1),
    ]
    for k, (src, dst, dr, dc) in enumerate(first):
        send(src, dst, e0_s.at[k], e0_r.at[k], dr, dc)

    def first_received(k):
        _, dst, dr, dc = first[k]
        received(dst, e0_s.at[k], e0_r.at[k], -dr, -dc)

    for l in range(1, 4):
        weights(l)
    for t in range(3):
        pltpu.make_async_copy(far.at[t], wf.at[0, :, :, pl.ds(t * CH, CH)], w_sem.at[4]).start()
        pltpu.make_async_copy(far.at[:, t], wf.at[1, :, :, pl.ds(t * CH, CH)], w_sem.at[5]).start()

    def weights_here(l):
        ref = w.at[l] if l < 4 else wf.at[l - 4]
        pltpu.make_async_copy(ref, ref, w_sem.at[l]).wait()

    def gain(l):
        return gains[l : l + 1, :][None]

    def mask(row, n):
        rows = row + lax.broadcasted_iota(jnp.int32, (n, WIDE, 1), 0)
        cols = lax.broadcasted_iota(jnp.int32, (n, WIDE, 1), 1)
        row_from = jnp.where(r == 0, 0, -8)
        row_to = jnp.where(r == nrow - 1, ROWS, ROWS + 8)
        col_from = jnp.where(c == ncol - 1, COLS + 8, COLS)
        col_to = jnp.where(c == 0, COLS + 8, WIDE)
        inside = (rows >= row_from) & (rows < row_to)
        inside = inside & ((cols < COLS) | ((cols >= col_from) & (cols < col_to)))
        return jnp.where(inside, 1.0, 0.0).astype(jnp.float32)

    def first_act(at, n):
        right = hr[pl.ds(at, n)].astype(jnp.float32)[:, :8]
        left = hl[pl.ds(at, n)].astype(jnp.float32)[:, 8:]
        halo = jnp.concatenate([right, left], axis=1)
        fx[pl.ds(at, n), COLS:] = halo.astype(jnp.bfloat16)
        value = jnp.concatenate([fx[pl.ds(at, n), :COLS].astype(jnp.float32), halo], axis=1)
        u0[pl.ds(at, n)] = norm_act(value, gain(0), None)

    def conv(u, at, d, l):
        left_side = jnp.concatenate(
            [u[pl.ds(at + a * d, R)].reshape(R * WIDE, CH) for a in range(3)], axis=-1
        )
        z = dot(left_side, w[l].reshape(3 * CH, 3 * CH))
        parts = [z[:, b * CH : (b + 1) * CH].reshape(R, WIDE, CH) for b in range(3)]
        return pltpu.roll(parts[0], d, 1) + parts[1] + pltpu.roll(parts[2], WIDE - d, 1)

    def layer0(row):
        new = fx[pl.ds(row + 3, R)].astype(jnp.float32) + conv(u0, row + 2, 1, 0)
        s[pl.ds(row + 2, R)] = new
        u1[pl.ds(row + 2, R)] = norm_act(new, gain(1), mask(row, R))

    def layer1(row):
        new = s[pl.ds(row + 2, R)] + conv(u1, row, 2, 1)
        s[pl.ds(row + 2, R)] = new
        u2[pl.ds(row + 4, R)] = norm_act(new, gain(2), mask(row, R))

    def layer2(row):
        new = s[pl.ds(row + 2, R), :COLS] + conv(u2, row, 4, 2)[:, :COLS]
        s[pl.ds(row + 2, R), :COLS] = new
        u3[pl.ds(row + 8, R)] = norm_act(new, gain(3), None)

    own_copy.wait()
    first_received(6)
    first_received(7)
    loop(4, lambda i: first_act(3 + R * i, R))
    weights_here(0)
    loop(3, lambda i: layer0(2 + R * i))
    for k in range(6):
        first_received(k)
    loop(2, lambda i: first_act(19 * i, 3))
    loop(2, lambda i: layer0(-2 + 16 * i))
    weights_here(1)
    loop(2, lambda i: layer1(12 * i))
    second = [
        (u2.at[pl.ds(4, 4)], u2.at[pl.ds(20, 4)], -1, 0),
        (u2.at[pl.ds(16, 4)], u2.at[pl.ds(0, 4)], 1, 0),
    ]
    for k, (src, dst, dr, dc) in enumerate(second):
        send(src, dst, e2_s.at[k], e2_r.at[k], dr, dc)
    loop(2, lambda i: layer1(4 + R * i))
    weights_here(2)
    loop(2, lambda i: layer2(4 + R * i))
    third = [
        (u3.at[pl.ds(16, 4)], u3.at[pl.ds(0, 4)], 1, 0),
        (u3.at[pl.ds(12, 4)], u3.at[pl.ds(28, 4)], -1, 0),
        (u3.at[pl.ds(20, 4)], u3.at[pl.ds(4, 4)], 1, 0),
        (u3.at[pl.ds(8, 4)], u3.at[pl.ds(24, 4)], -1, 0),
    ]
    for k in (0, 1):
        src, dst, dr, dc = third[k]
        send(src, dst, e3_s.at[k], e3_r.at[k], dr, dc)
    for k, (src, dst, dr, dc) in enumerate(second):
        received(dst, e2_s.at[k], e2_r.at[k], -dr, -dc)
    loop(2, lambda i: layer2(12 * i))
    for k in (2, 3):
        src, dst, dr, dc = third[k]
        send(src, dst, e3_s.at[k], e3_r.at[k], dr, dc)

    def spread_cols(z):
        z = [z[:, b * CH : (b + 1) * CH].reshape(R, COLS, CH) for b in range(3)]
        none = jnp.zeros((R, 8, CH), jnp.float32)
        here = (
            jnp.concatenate([none, z[0][:, : COLS - 8]], axis=1)
            + z[1]
            + jnp.concatenate([z[2][:, 8:], none], axis=1)
        )
        return here, z[0][:, COLS - 8 :], z[2][:, :8]

    def add(row, value):
        s[pl.ds(row + 2, R), :COLS] = s[pl.ds(row + 2, R), :COLS] + value

    def layer3_own(i):
        row = R * i
        low_row = lax.rem(row, 8)
        left_side = jnp.concatenate(
            [u3[pl.ds(8 + low_row + 8 * a, R)].reshape(R * COLS, CH) for a in range(2)], axis=-1
        )
        z = dot(left_side, w[3, pl.ds(1 - row // 8, 2)].reshape(2 * CH, 3 * CH))
        here, to_right, to_left = spread_cols(z)
        add(row, here)
        edge[i, 0] = to_right
        edge[i, 1] = to_left

    def row_of(k):
        even, late = 1 - lax.rem(k, 2), k // 2
        return even * 4 * late + (1 - even) * (12 - 4 * late)

    def layer3_halo(k):
        odd = lax.rem(k, 2)
        row = row_of(k)
        at = row + 16 * odd
        place = u3.at[pl.ds(at, R)]

        @pl.when(odd == 0)
        def _():
            received(place, e3_s.at[k], e3_r.at[k], -1, 0)

        @pl.when(odd == 1)
        def _():
            received(place, e3_s.at[k], e3_r.at[k], 1, 0)

        z = dot(u3[pl.ds(at, R)].reshape(R * COLS, CH), w[3, 2 * odd])
        here, to_right, to_left = spread_cols(z)
        add(row, here)
        i = row // R
        edge_out[k, 0] = (edge[i, 0] + to_right).reshape(R * 8, CH).astype(jnp.bfloat16)
        edge_out[k, 1] = (edge[i, 1] + to_left).reshape(R * 8, CH).astype(jnp.bfloat16)
        send(edge_out.at[k, 0], edge_in.at[k, 0], ed_s.at[k, 0], ed_r.at[k, 0], 0, 1)
        send(edge_out.at[k, 1], edge_in.at[k, 1], ed_s.at[k, 1], ed_r.at[k, 1], 0, -1)

    def move(k, first_axis, action, buf_out, buf_in, ss, rs):
        for parity in range(2):
            dr, dc = (0, 1) if (parity == 0) == first_axis else (HOP, 0)

            @pl.when(lax.rem(k, 2) == parity)
            def _():
                for side, sign in ((0, 1), (1, -1)):
                    if action == "received":
                        received(buf_in.at[k, side], ss.at[k, side], rs.at[k, side], -sign * dr, -sign * dc)
                    else:
                        fn = send if action == "send" else sent
                        src = buf_out.at[k] if first_axis else buf_out.at[k, side]
                        fn(src, buf_in.at[k, side], ss.at[k, side], rs.at[k, side], sign * dr, sign * dc)

    def layer3_end(k):
        row = row_of(k)
        received(edge_in.at[k, 0], ed_s.at[k, 0], ed_r.at[k, 0], 0, -1)
        received(edge_in.at[k, 1], ed_s.at[k, 1], ed_r.at[k, 1], 0, 1)
        old = s[pl.ds(row + 2, R), :COLS]
        from_left = edge_in[k, 0].astype(jnp.float32).reshape(R, 8, CH)
        from_right = edge_in[k, 1].astype(jnp.float32).reshape(R, 8, CH)
        new = jnp.concatenate(
            [old[:, :8] + from_left, old[:, 8 : COLS - 8], old[:, COLS - 8 :] + from_right], axis=1
        )
        s[pl.ds(row + 2, R), :COLS] = new
        fa[k] = norm_act(new, gain(4), None)
        move(k, True, "send", fa, fr, fa_s, fa_r)

    weights_here(3)
    loop(4, layer3_own)
    weights_here(4)
    weights_here(5)

    def layer3_pair(g):
        loop(2, lambda j: layer3_halo(2 * g + j))
        loop(2, lambda j: layer3_end(2 * g + j))

    loop(2, layer3_pair)

    def far_step(k):
        row = row_of(k)
        move(k, True, "received", fa, fr, fa_s, fa_r)
        left_side = jnp.concatenate(
            [v.reshape(R * COLS, CH) for v in (fr[k, 0], fa[k], fr[k, 1])], axis=-1
        )
        z = dot(left_side, wf[lax.rem(k, 2)].reshape(3 * CH, 3 * CH))
        fp[k, 0] = z[:, :CH].astype(jnp.bfloat16).reshape(R, COLS, CH)
        fp[k, 1] = z[:, 2 * CH :].astype(jnp.bfloat16).reshape(R, COLS, CH)
        move(k, False, "send", fp, fq, fp_s, fp_r)
        add(row, z[:, CH : 2 * CH].reshape(R, COLS, CH))

    loop(4, far_step)

    def out_copy(k):
        row = row_of(k)
        return pltpu.make_async_copy(s.at[pl.ds(row + 2, R), pl.ds(0, COLS)], out.at[pl.ds(row, R)], o_sem.at[k])

    def far_end(k):
        move(k, False, "received", fp, fq, fp_s, fp_r)
        add(row_of(k), fq[k, 0].astype(jnp.float32) + fq[k, 1].astype(jnp.float32))
        out_copy(k).start()

    loop(4, far_end)

    for k, (src, dst, dr, dc) in enumerate(first):
        sent(src, dst, e0_s.at[k], e0_r.at[k], dr, dc)
    for k, (src, dst, dr, dc) in enumerate(second):
        sent(src, dst, e2_s.at[k], e2_r.at[k], dr, dc)
    for k, (src, dst, dr, dc) in enumerate(third):
        sent(src, dst, e3_s.at[k], e3_r.at[k], dr, dc)

    def all_sent(k):
        sent(edge_out.at[k, 0], edge_in.at[k, 0], ed_s.at[k, 0], ed_r.at[k, 0], 0, 1)
        sent(edge_out.at[k, 1], edge_in.at[k, 1], ed_s.at[k, 1], ed_r.at[k, 1], 0, -1)
        move(k, True, "sent", fa, fr, fa_s, fa_r)
        move(k, False, "sent", fp, fq, fp_s, fp_r)
        out_copy(k).wait()

    loop(4, all_sent)


def local(nrow, ncol, features, inner_weights, far_weights, gains):
    bf16, f32 = jnp.bfloat16, jnp.float32
    dma = pltpu.SemaphoreType.DMA
    hbm = pl.BlockSpec(memory_space=pl.ANY)
    return pl.pallas_call(
        functools.partial(kernel, nrow, ncol),
        out_shape=jax.ShapeDtypeStruct(features.shape, f32),
        in_specs=[hbm, hbm, hbm, pl.BlockSpec(memory_space=pltpu.VMEM)],
        out_specs=hbm,
        scratch_shapes=[
            pltpu.VMEM((ROWS + 6, WIDE, CH), bf16),
            pltpu.VMEM((ROWS + 6, 16, CH), bf16),
            pltpu.VMEM((ROWS + 6, 16, CH), bf16),
            pltpu.VMEM((ROWS + 6, WIDE, CH), bf16),
            pltpu.VMEM((ROWS + 4, WIDE, CH), bf16),
            pltpu.VMEM((ROWS + 8, WIDE, CH), bf16),
            pltpu.VMEM((ROWS + 16, COLS, CH), bf16),
            pltpu.VMEM((ROWS + 4, WIDE, CH), f32),
            pltpu.VMEM((4, 3, CH, 3 * CH), bf16),
            pltpu.VMEM((2, 3, CH, 3 * CH), bf16),
            pltpu.VMEM((4, 2, R, 8, CH), f32),
            pltpu.VMEM((4, 2, R * 8, CH), bf16),
            pltpu.VMEM((4, 2, R * 8, CH), bf16),
            pltpu.VMEM((4, R, COLS, CH), bf16),
            pltpu.VMEM((4, 2, R, COLS, CH), bf16),
            pltpu.VMEM((4, 2, R, COLS, CH), bf16),
            pltpu.VMEM((4, 2, R, COLS, CH), bf16),
            dma, dma((6,)), dma((4,)),
            dma((8,)), dma((8,)), dma((2,)), dma((2,)), dma((4,)), dma((4,)),
            dma((4, 2)), dma((4, 2)), dma((4, 2)), dma((4, 2)), dma((4, 2)), dma((4, 2)),
        ],
        compiler_params=pltpu.CompilerParams(
            collective_id=0, has_side_effects=True, vmem_limit_bytes=56 * 2**20
        ),
    )(features, inner_weights, far_weights, gains)


def solution(mesh):
    return jax.shard_map(
        functools.partial(local, mesh.shape["row"], mesh.shape["col"]),
        mesh=mesh,
        in_specs=(P("row", "col", None), P(), P(), P()),
        out_specs=P("row", "col", None),
        check_vma=False,
    )
```

profile of v0, /device:TPU:216, one launch (start us, length us, event | category | flops | bytes accessed | tf_op | source)
XLA Modules:
  0.0 75.2 jit_solution(1117871840636986650)
XLA Ops:
  0.0 72.5 %shard_map.46 = f32[16,64,384]{2,1,0:T(8,128)} custom-call(bf16[16,64,384]{2,1,0:T(8,128)(2,1)} %feat.1, bf16[4,3,3,384,384]{4,3,2,1,0:T(8,128)(2,1)} %inner.1, bf16[3,3,384,384]{3,2,1,0:T(8,128)(2,1)} %far.1, f32[5,384]{1,0:T(8,128)} %gains.1), custom_call_target="tpu_custom_call" | custom-call | tf_op jit(solution)/shard_map/pallas_call | solution.py:386
  72.5 2.7 %copy.6 = f32[16,64,384]{2,1,0:T(8,128)} copy(f32[16,64,384]{2,1,0:T(8,128)} %shard_map.46) | data formatting | bytes 3145728
where the time goes:
time: 75.3 us; the launch traced here: 75.2 us
  Pallas kernels  72.5 us (96%)
  local copies, waits for them, and re-layouts  2.7 us (4%)
    pallas_call x1, Pallas kernels, local(): pl.pallas_call(functools.partial(kernel, nrow, ncol), out_shape=jax.Shape...  72.5 us
    unnamed x1, local copies, waits for them, and re-layouts  2.7 us

commit v1 on v0

v1 whole, which is shorter than its diff:
```python
import functools

import jax
import jax.numpy as jnp
from jax import lax
from jax.experimental import pallas as pl
from jax.experimental.pallas import tpu as pltpu
from jax.sharding import PartitionSpec as P

MESH = pl.DeviceIdType.MESH
CH = 384
HOP = 4
ROWS, COLS = 16, 64
WIDE = 80
R = 4


def norm_act(stream, gain, mask):
    centre = jnp.mean(stream, axis=-1, keepdims=True)
    moved = stream - centre
    spread = jnp.mean(moved * moved, axis=-1, keepdims=True)
    scale = lax.rsqrt(spread + 1e-05)
    if mask is not None:
        scale = scale * mask
    return jax.nn.gelu(moved * scale * gain).astype(jnp.bfloat16)


def dot(a, b):
    return jnp.dot(a, b, preferred_element_type=jnp.float32)


def row8(row):
    return row * 8 if isinstance(row, int) else pl.multiple_of(row * 8, 32)


def unrolled(n, body):
    for i in range(n):
        body(i)


def loop(n, body):
    def step(i, carry):
        body(i)
        return carry

    lax.fori_loop(0, n, step, 0)


def kernel(
    nrow, ncol,
    feat, inner, far, gains, out,
    fx, pk, hb, u0, u1, u2, u3, pk3, hb3, s, zh, w, wf,
    fa, fr, fp, fq,
    in_sem, w_sem, o_sem,
    e0_s, e0_r, e2_s, e2_r, e3_s, e3_r, x3_s, x3_r, d3_s, d3_r, fa_s, fa_r, fp_s, fp_r,
):
    r, c = lax.axis_index("row"), lax.axis_index("col")

    def there(dr, dc):
        return (r + dr >= 0) & (r + dr < nrow) & (c + dc >= 0) & (c + dc < ncol)

    def remote(src, dst, ss, rs, dr, dc):
        return pltpu.make_async_remote_copy(
            src_ref=src, dst_ref=dst, send_sem=ss, recv_sem=rs,
            device_id=(r + dr, c + dc), device_id_type=MESH,
        )

    def send(src, dst, ss, rs, dr, dc):
        @pl.when(there(dr, dc))
        def _():
            remote(src, dst, ss, rs, dr, dc).start()

    def sent(src, dst, ss, rs, dr, dc):
        @pl.when(there(dr, dc))
        def _():
            remote(src, dst, ss, rs, dr, dc).wait_send()

    def received(dst, ss, rs, dr, dc):
        @pl.when(there(dr, dc))
        def _():
            remote(dst, dst, ss, rs, dr, dc).wait_recv()

    own_copy = pltpu.make_async_copy(feat, fx.at[pl.ds(4, ROWS), pl.ds(0, COLS)], in_sem)
    own_copy.start()

    def weights(l):
        for b in range(3):
            pltpu.make_async_copy(
                inner.at[l, :, b], w.at[l, :, :, pl.ds(b * CH, CH)], w_sem.at[l]
            ).start()

    weights(0)

    greet = [(dr, dc) for dr in (-1, 0, 1) for dc in (-1, 0, 1) if dr or dc] + [(HOP, 0), (-HOP, 0)]
    barrier = pltpu.get_barrier_semaphore()
    for dr, dc in greet:
        @pl.when(there(dr, dc))
        def _():
            pl.semaphore_signal(barrier, inc=1, device_id=(r + dr, c + dc), device_id_type=MESH)


    @pl.when(r == 0)
    def _():
        fx[0:4, :COLS] = jnp.zeros((4, COLS, CH), fx.dtype)
        u2[0:4] = jnp.zeros((4, WIDE, CH), u2.dtype)
        u3[0:8] = jnp.zeros((8, COLS, CH), u3.dtype)
        for side in range(2):
            hb[side, 0:32] = jnp.zeros((32, CH), hb.dtype)
            hb3[side, 0:64] = jnp.zeros((64, CH), hb3.dtype)

    @pl.when(r == nrow - 1)
    def _():
        fx[20:24, :COLS] = jnp.zeros((4, COLS, CH), fx.dtype)
        u2[20:24] = jnp.zeros((4, WIDE, CH), u2.dtype)
        u3[24:32] = jnp.zeros((8, COLS, CH), u3.dtype)
        for side in range(2):
            hb[side, 160:192] = jnp.zeros((32, CH), hb.dtype)
            hb3[side, 192:256] = jnp.zeros((64, CH), hb3.dtype)

    tile_zero = jnp.zeros((R, COLS, CH), jnp.bfloat16)

    @pl.when(c == 0)
    def _():
        hb[1] = jnp.zeros((192, CH), hb.dtype)
        hb3[1] = jnp.zeros((256, CH), hb3.dtype)
        for k in range(4):
            (fr if k % 2 == 0 else fq)[k, 0] = tile_zero

    @pl.when(c == ncol - 1)
    def _():
        hb[0] = jnp.zeros((192, CH), hb.dtype)
        hb3[0] = jnp.zeros((256, CH), hb3.dtype)
        for k in range(4):
            (fr if k % 2 == 0 else fq)[k, 1] = tile_zero

    @pl.when(r < HOP)
    def _():
        for k in range(4):
            (fr if k % 2 == 1 else fq)[k, 0] = tile_zero

    @pl.when(r >= nrow - HOP)
    def _():
        for k in range(4):
            (fr if k % 2 == 1 else fq)[k, 1] = tile_zero

    def gain(l):
        return gains[l : l + 1, :][None]

    def flat(value):
        n = value.shape[0]
        return value.reshape(n * 8, CH).astype(jnp.bfloat16)

    def unflat(ref, side, row, n):
        at = pl.multiple_of(row * 8, 16)
        return ref[side, pl.ds(at, n * 8)].astype(jnp.float32).reshape(n, 8, CH)

    def own_act(i):
        row = R * i
        value = fx[pl.ds(row + 4, R), :COLS].astype(jnp.float32)
        at = pl.ds(row8(row), R * 8)
        pk[0, at] = flat(value[:, :8])
        pk[1, at] = flat(value[:, COLS - 8 :])
        u0[pl.ds(row + 4, R), :COLS] = norm_act(value, gain(0), None)

    own_copy.wait()
    loop(4, own_act)
    pl.semaphore_wait(barrier, sum(jnp.where(there(dr, dc), 1, 0) for dr, dc in greet))

    own = pl.ds(0, COLS)
    top, mid, bottom = pl.ds(0, 32), pl.ds(32, ROWS * 8), pl.ds(160, 32)
    head, tail = pl.ds(0, 32), pl.ds(96, 32)
    first = [
        (feat.at[pl.ds(0, 3)], fx.at[pl.ds(20, 3), own], -1, 0),
        (feat.at[pl.ds(13, 3)], fx.at[pl.ds(1, 3), own], 1, 0),
        (pk.at[0, head], hb.at[0, bottom], -1, -1),
        (pk.at[1, head], hb.at[1, bottom], -1, 1),
        (pk.at[0, tail], hb.at[0, top], 1, -1),
        (pk.at[1, tail], hb.at[1, top], 1, 1),
        (pk.at[0], hb.at[0, mid], 0, -1),
        (pk.at[1], hb.at[1, mid], 0, 1),
    ]
    for k, (src, dst, dr, dc) in enumerate(first):
        send(src, dst, e0_s.at[k], e0_r.at[k], dr, dc)

    def first_received(k):
        _, dst, dr, dc = first[k]
        received(dst, e0_s.at[k], e0_r.at[k], -dr, -dc)

    for l in range(1, 4):
        weights(l)
    for t in range(3):
        pltpu.make_async_copy(far.at[t], wf.at[0, :, :, pl.ds(t * CH, CH)], w_sem.at[4]).start()
        pltpu.make_async_copy(far.at[:, t], wf.at[1, :, :, pl.ds(t * CH, CH)], w_sem.at[5]).start()

    def weights_here(l):
        ref = w.at[l] if l < 4 else wf.at[l - 4]
        pltpu.make_async_copy(ref, ref, w_sem.at[l]).wait()

    def mask(row, n):
        rows = row + lax.broadcasted_iota(jnp.int32, (n, WIDE, 1), 0)
        cols = lax.broadcasted_iota(jnp.int32, (n, WIDE, 1), 1)
        row_from = jnp.where(r == 0, 0, -8)
        row_to = jnp.where(r == nrow - 1, ROWS, ROWS + 8)
        col_from = jnp.where(c == ncol - 1, COLS + 8, COLS)
        col_to = jnp.where(c == 0, COLS + 8, WIDE)
        inside = (rows >= row_from) & (rows < row_to)
        inside = inside & ((cols < COLS) | ((cols >= col_from) & (cols < col_to)))
        return jnp.where(inside, 1.0, 0.0).astype(jnp.float32)

    def halo_cols(row, n):
        return jnp.concatenate([unflat(hb, 0, row + 4, n), unflat(hb, 1, row + 4, n)], axis=1)

    def halo_act(i):
        row = R * i
        halo = halo_cols(row, R)
        fx[pl.ds(row + 4, R), COLS:] = halo.astype(jnp.bfloat16)
        u0[pl.ds(row + 4, R), COLS:] = norm_act(halo, gain(0), None)

    def outer_act(i):
        row = 20 * i - 4
        halo = halo_cols(row, R)
        fx[pl.ds(row + 4, R), COLS:] = halo.astype(jnp.bfloat16)
        value = jnp.concatenate([fx[pl.ds(row + 4, R), :COLS].astype(jnp.float32), halo], axis=1)
        u0[pl.ds(row + 4, R)] = norm_act(value, gain(0), None)

    def shifted(parts, d):
        return pltpu.roll(parts[0], d, 1) + parts[1] + pltpu.roll(parts[2], WIDE - d, 1)

    def layer0_own(row):
        left_side = jnp.concatenate(
            [u0[pl.ds(row + 3 + a, R), :COLS].reshape(R * COLS, CH) for a in range(3)], axis=-1
        )
        z = dot(left_side, w[0].reshape(3 * CH, 3 * CH))
        none = jnp.zeros((R, WIDE - COLS, CH), jnp.float32)
        parts = [
            jnp.concatenate([z[:, b * CH : (b + 1) * CH].reshape(R, COLS, CH), none], axis=1)
            for b in range(3)
        ]
        s[pl.ds(row + 2, R)] = shifted(parts, 1)

    def layer0_halo_dot():
        n = 3 * R
        left_side = jnp.concatenate(
            [u0[pl.ds(5 + a, n), COLS:].reshape(n * 16, CH) for a in range(3)], axis=-1
        )
        zh[...] = dot(left_side, w[0].reshape(3 * CH, 3 * CH)).reshape(n, 16, 3 * CH)

    def layer0_halo(i):
        row = 2 + R * i
        z = zh[pl.ds(R * i, R)]
        none = jnp.zeros((R, COLS, CH), jnp.float32)
        parts = [jnp.concatenate([none, z[:, :, b * CH : (b + 1) * CH]], axis=1) for b in range(3)]
        new = fx[pl.ds(row + 4, R)].astype(jnp.float32) + s[pl.ds(row + 2, R)] + shifted(parts, 1)
        s[pl.ds(row + 2, R)] = new
        u1[pl.ds(row + 2, R)] = norm_act(new, gain(1), mask(row, R))

    def conv(u, at, d, l):
        left_side = jnp.concatenate(
            [u[pl.ds(at + a * d, R)].reshape(R * WIDE, CH) for a in range(3)], axis=-1
        )
        z = dot(left_side, w[l].reshape(3 * CH, 3 * CH))
        parts = [z[:, b * CH : (b + 1) * CH].reshape(R, WIDE, CH) for b in range(3)]
        return shifted(parts, d)

    def layer0(row):
        new = fx[pl.ds(row + 4, R)].astype(jnp.float32) + conv(u0, row + 3, 1, 0)
        s[pl.ds(row + 2, R)] = new
        u1[pl.ds(row + 2, R)] = norm_act(new, gain(1), mask(row, R))

    def layer1(row):
        new = s[pl.ds(row + 2, R)] + conv(u1, row, 2, 1)
        s[pl.ds(row + 2, R)] = new
        u2[pl.ds(row + 4, R)] = norm_act(new, gain(2), mask(row, R))

    def layer2(row):
        new = s[pl.ds(row + 2, R), :COLS] + conv(u2, row, 4, 2)[:, :COLS]
        s[pl.ds(row + 2, R), :COLS] = new
        act = norm_act(new, gain(3), None)
        u3[pl.ds(row + 8, R)] = act
        at = pl.ds(row8(row), R * 8)
        act = act.astype(jnp.float32)
        pk3[0, at] = flat(act[:, :8])
        pk3[1, at] = flat(act[:, COLS - 8 :])

    weights_here(0)
    loop(3, lambda i: layer0_own(2 + R * i))
    first_received(6)
    first_received(7)
    loop(4, halo_act)
    layer0_halo_dot()
    loop(3, layer0_halo)
    for k in range(6):
        first_received(k)
    loop(2, outer_act)
    unrolled(2, lambda i: layer0(-2 + 16 * i))
    weights_here(1)
    unrolled(2, lambda i: layer1(12 * i))
    second = [
        (u2.at[pl.ds(4, 4)], u2.at[pl.ds(20, 4)], -1, 0),
        (u2.at[pl.ds(16, 4)], u2.at[pl.ds(0, 4)], 1, 0),
    ]
    for k, (src, dst, dr, dc) in enumerate(second):
        send(src, dst, e2_s.at[k], e2_r.at[k], dr, dc)
    unrolled(2, lambda i: layer1(4 + R * i))
    weights_here(2)
    unrolled(2, lambda i: layer2(4 + R * i))
    third = [
        (u3.at[pl.ds(16, 4)], u3.at[pl.ds(0, 4)], 1, 0),
        (u3.at[pl.ds(12, 4)], u3.at[pl.ds(28, 4)], -1, 0),
        (u3.at[pl.ds(20, 4)], u3.at[pl.ds(4, 4)], 1, 0),
        (u3.at[pl.ds(8, 4)], u3.at[pl.ds(24, 4)], -1, 0),
    ]
    third_from = (8, 4, 12, 0)
    third_to = (-8, 20, -4, 16)

    def columns(k):
        for side, dc in ((0, -1), (1, 1)):
            src = pk3.at[side, pl.ds(third_from[k] * 8, 32)]
            here = hb3.at[side, pl.ds((third_from[k] + 8) * 8, 32)]
            corner = hb3.at[side, pl.ds((third_to[k] + 8) * 8, 32)]
            yield src, here, x3_s.at[k, side], x3_r.at[k, side], 0, dc
            yield src, corner, d3_s.at[k, side], d3_r.at[k, side], third[k][2], dc

    def third_send(k):
        src, dst, dr, dc = third[k]
        send(src, dst, e3_s.at[k], e3_r.at[k], dr, dc)
        for args in columns(k):
            send(*args)

    third_send(0)
    third_send(1)
    for k, (src, dst, dr, dc) in enumerate(second):
        received(dst, e2_s.at[k], e2_r.at[k], -dr, -dc)
    unrolled(2, lambda i: layer2(12 * i))
    third_send(2)
    third_send(3)

    def spread_cols(z):
        z = [z[:, b * CH : (b + 1) * CH].reshape(R, COLS, CH) for b in range(3)]
        none = jnp.zeros((R, 8, CH), jnp.float32)
        return (
            jnp.concatenate([none, z[0][:, : COLS - 8]], axis=1)
            + z[1]
            + jnp.concatenate([z[2][:, 8:], none], axis=1)
        )

    def add(row, value):
        s[pl.ds(row + 2, R), :COLS] = s[pl.ds(row + 2, R), :COLS] + value

    def layer3_own(i):
        row = R * i
        low_row = lax.rem(row, 8)
        left_side = jnp.concatenate(
            [u3[pl.ds(8 + low_row + 8 * a, R)].reshape(R * COLS, CH) for a in range(2)], axis=-1
        )
        z = dot(left_side, w[3, pl.ds(1 - row // 8, 2)].reshape(2 * CH, 3 * CH))
        add(row, spread_cols(z))

    def row_of(k):
        even, late = 1 - lax.rem(k, 2), k // 2
        return even * 4 * late + (1 - even) * (12 - 4 * late)

    def move(k, first_axis, action, buf_out, buf_in, ss, rs):
        for parity in range(2):
            dr, dc = (0, 1) if (parity == 0) == first_axis else (HOP, 0)

            @pl.when(lax.rem(k, 2) == parity)
            def _():
                for side, sign in ((0, 1), (1, -1)):
                    if action == "received":
                        received(buf_in.at[k, side], ss.at[k, side], rs.at[k, side], -sign * dr, -sign * dc)
                    else:
                        fn = send if action == "send" else sent
                        src = buf_out.at[k] if first_axis else buf_out.at[k, side]
                        fn(src, buf_in.at[k, side], ss.at[k, side], rs.at[k, side], sign * dr, sign * dc)

    def column_taps(side, rows):
        left_side = jnp.concatenate(
            [
                jnp.concatenate(
                    [hb3[side, pl.ds(pl.multiple_of((row + 8 * a) * 8, 32), R * 8)] for a in range(3)],
                    axis=-1,
                )
                for row in rows
            ],
            axis=0,
        )
        b = 2 if side == 0 else 0
        return dot(left_side, w[3, :, :, b * CH : (b + 1) * CH].reshape(3 * CH, CH))

    def layer3_pair(g):
        rows = (R * g, 12 - R * g)
        from_right = column_taps(0, rows)
        from_left = column_taps(1, rows)
        for odd in range(2):
            k, row = 2 * g + odd, rows[odd]
            z = dot(u3[pl.ds(row + 16 * odd, R)].reshape(R * COLS, CH), w[3, 2 * odd])
            new = s[pl.ds(row + 2, R), :COLS] + spread_cols(z)
            part = slice(odd * R * 8, (odd + 1) * R * 8)
            new = jnp.concatenate(
                [
                    new[:, :8] + from_left[part].reshape(R, 8, CH),
                    new[:, 8 : COLS - 8],
                    new[:, COLS - 8 :] + from_right[part].reshape(R, 8, CH),
                ],
                axis=1,
            )
            s[pl.ds(row + 2, R), :COLS] = new
            fa[k] = norm_act(new, gain(4), None)

    def third_received(k):
        src, dst, dr, dc = third[k]
        received(dst, e3_s.at[k], e3_r.at[k], -dr, -dc)
        for (_, dst, ss, rs, dr, dc) in list(columns(k))[1::2]:
            received(dst, ss, rs, -dr, -dc)

    weights_here(3)
    loop(4, layer3_own)
    weights_here(4)
    weights_here(5)

    for k in range(4):
        for (_, dst, ss, rs, dr, dc) in list(columns(k))[0::2]:
            received(dst, ss, rs, -dr, -dc)

    def far_send(k):
        move(k, True, "send", fa, fr, fa_s, fa_r)

    def far_sent(k):
        move(k, True, "sent", fa, fr, fa_s, fa_r)

    def layer3_turn(g):
        for turn in range(2):
            @pl.when(g == turn)
            def _():
                third_received(2 * turn)
                third_received(2 * turn + 1)

        layer3_pair(g)

    loop(2, layer3_turn)
    for k in (0, 1):
        far_send(k)
    for k in (0, 1):
        far_sent(k)
    for k in (2, 3):
        far_send(k)

    def far_step(k):
        row = row_of(k)
        move(k, True, "received", fa, fr, fa_s, fa_r)
        left_side = jnp.concatenate(
            [v.reshape(R * COLS, CH) for v in (fr[k, 0], fa[k], fr[k, 1])], axis=-1
        )
        z = dot(left_side, wf[lax.rem(k, 2)].reshape(3 * CH, 3 * CH))
        fp[k, 0] = z[:, :CH].astype(jnp.bfloat16).reshape(R, COLS, CH)
        fp[k, 1] = z[:, 2 * CH :].astype(jnp.bfloat16).reshape(R, COLS, CH)
        move(k, False, "send", fp, fq, fp_s, fp_r)
        add(row, z[:, CH : 2 * CH].reshape(R, COLS, CH))

    loop(4, far_step)

    def out_copy(k):
        row = row_of(k)
        return pltpu.make_async_copy(s.at[pl.ds(row + 2, R), pl.ds(0, COLS)], out.at[pl.ds(row, R)], o_sem.at[k])

    def far_end(k):
        move(k, False, "received", fp, fq, fp_s, fp_r)
        add(row_of(k), fq[k, 0].astype(jnp.float32) + fq[k, 1].astype(jnp.float32))
        out_copy(k).start()

    loop(4, far_end)

    for k, (src, dst, dr, dc) in enumerate(first):
        sent(src, dst, e0_s.at[k], e0_r.at[k], dr, dc)
    for k, (src, dst, dr, dc) in enumerate(second):
        sent(src, dst, e2_s.at[k], e2_r.at[k], dr, dc)
    for k, (src, dst, dr, dc) in enumerate(third):
        sent(src, dst, e3_s.at[k], e3_r.at[k], dr, dc)
        for args in columns(k):
            sent(*args)

    def all_sent(k):
        @pl.when(k >= 2)
        def _():
            far_sent(k)

        move(k, False, "sent", fp, fq, fp_s, fp_r)
        out_copy(k).wait()

    loop(4, all_sent)


def local(nrow, ncol, features, inner_weights, far_weights, gains):
    bf16, f32 = jnp.bfloat16, jnp.float32
    dma = pltpu.SemaphoreType.DMA
    hbm = pl.BlockSpec(memory_space=pl.ANY)
    return pl.pallas_call(
        functools.partial(kernel, nrow, ncol),
        out_shape=jax.ShapeDtypeStruct(features.shape, f32),
        in_specs=[hbm, hbm, hbm, pl.BlockSpec(memory_space=pltpu.VMEM)],
        out_specs=hbm,
        scratch_shapes=[
            pltpu.VMEM((ROWS + 8, WIDE, CH), bf16),
            pltpu.VMEM((2, ROWS * 8, CH), bf16),
            pltpu.VMEM((2, (ROWS + 8) * 8, CH), bf16),
            pltpu.VMEM((ROWS + 8, WIDE, CH), bf16),
            pltpu.VMEM((ROWS + 4, WIDE, CH), bf16),
            pltpu.VMEM((ROWS + 8, WIDE, CH), bf16),
            pltpu.VMEM((ROWS + 16, COLS, CH), bf16),
            pltpu.VMEM((2, ROWS * 8, CH), bf16),
            pltpu.VMEM((2, (ROWS + 16) * 8, CH), bf16),
            pltpu.VMEM((ROWS + 4, WIDE, CH), f32),
            pltpu.VMEM((3 * R, 16, 3 * CH), f32),
            pltpu.VMEM((4, 3, CH, 3 * CH), bf16),
            pltpu.VMEM((2, 3, CH, 3 * CH), bf16),
            pltpu.VMEM((4, R, COLS, CH), bf16),
            pltpu.VMEM((4, 2, R, COLS, CH), bf16),
            pltpu.VMEM((4, 2, R, COLS, CH), bf16),
            pltpu.VMEM((4, 2, R, COLS, CH), bf16),
            dma, dma((6,)), dma((4,)),
            dma((8,)), dma((8,)), dma((2,)), dma((2,)), dma((4,)), dma((4,)),
            dma((4, 2)), dma((4, 2)), dma((4, 2)), dma((4, 2)), dma((4, 2)), dma((4, 2)), dma((4, 2)), dma((4, 2)),
        ],
        compiler_params=pltpu.CompilerParams(
            collective_id=0, has_side_effects=True, vmem_limit_bytes=50 * 2**20
        ),
    )(features, inner_weights, far_weights, gains)


def solution(mesh):
    return jax.shard_map(
        functools.partial(local, mesh.shape["row"], mesh.shape["col"]),
        mesh=mesh,
        in_specs=(P("row", "col", None), P(), P(), P()),
        out_specs=P("row", "col", None),
        check_vma=False,
    )
```

time: 75.3 us -> 68 us (0.903)
  the two profiles are of different devices: /device:TPU:216 before, /device:TPU:233 now
where the time goes in v1:
time: 68 us; the launch traced here: 67.3 us
  Pallas kernels  64.3 us (95%)
  local copies, waits for them, and re-layouts  2.98 us (4%)
    pallas_call x1, Pallas kernels, local(): pl.pallas_call(functools.partial(kernel, nrow, ncol), out_shape=jax.Shape...  64.3 us
    unnamed x5, local copies, waits for them, and re-layouts  2.98 us

profile of v1, /device:TPU:233, one launch (start us, length us, event | category | flops | bytes accessed | tf_op | source)
XLA Modules:
  0.0 67.3 jit_solution(12560416869431884026)
XLA Ops:
  0.0 0.0 copy-start
  0.0 1.1 %copy-done = bf16[16,64,384]{2,1,0:T(8,128)(2,1)S(1)} copy-done((bf16[16,64,384]{2,1,0:T(8,128)(2,1)S(1)}, bf16[16,64,384]{2,1,0:T(8,128)(2,1)}, u32[]{:S(2)}) %copy-start) | copy-done | bytes 786456
  1.1 0.0 copy-start.1
  1.1 0.7 %copy-done.1 = f32[5,384]{1,0:T(8,128)S(1)} copy-done((f32[5,384]{1,0:T(8,128)S(1)}, f32[5,384]{1,0:T(8,128)}, u32[]{:S(2)}) %copy-start.1) | copy-done | bytes 7704
  1.8 64.3 %shard_map.46 = f32[16,64,384]{2,1,0:T(8,128)S(1)} custom-call(bf16[16,64,384]{2,1,0:T(8,128)(2,1)S(1)} %copy-done, bf16[4,3,3,384,384]{4,3,2,1,0:T(8,128)(2,1)} %inner.1, bf16[3,3,384,384]{3,2,1,0:T(8,128)(2,1)} %far.1, f32[5,384]{1,0:T(8,128)S(1)} %copy-done.1), custom_call_target="tpu_custom_call" | custom-call | tf_op jit(solution)/shard_map/pallas_call | solution.py:498
  66.1 1.1 %copy.6 = f32[16,64,384]{2,1,0:T(8,128)} copy(f32[16,64,384]{2,1,0:T(8,128)S(1)} %shard_map.46) | data formatting | bytes 3145728
Async XLA Ops:
  0.0 1.1 %copy-start = (bf16[16,64,384]{2,1,0:T(8,128)(2,1)S(1)}, bf16[16,64,384]{2,1,0:T(8,128)(2,1)}, u32[]{:S(2)}) copy-start(bf16[16,64,384]{2,1,0:T(8,128)(2,1)} %feat.1) | copy-start | bytes 2359300
  1.1 0.7 %copy-start.1 = (f32[5,384]{1,0:T(8,128)S(1)}, f32[5,384]{1,0:T(8,128)}, u32[]{:S(2)}) copy-start(f32[5,384]{1,0:T(8,128)} %gains.1) | copy-start | bytes 23044

commit v2 on v1

--- a/solution.py
+++ b/solution.py
@@ -48,10 +48,10 @@
 
 def kernel(
     nrow, ncol,
-    feat, inner, far, gains, out,
-    fx, pk, hb, u0, u1, u2, u3, pk3, hb3, s, zh, w, wf,
+    feat, inner, far, gains_in, out,
+    gains, fx, pk, hb, u0, u1, u2, u3, pk3, hb3, s, zh, w, wf,
     fa, fr, fp, fq,
-    in_sem, w_sem, o_sem,
+    in_sem, g_sem, w_sem,
     e0_s, e0_r, e2_s, e2_r, e3_s, e3_r, x3_s, x3_r, d3_s, d3_r, fa_s, fa_r, fp_s, fp_r,
 ):
     r, c = lax.axis_index("row"), lax.axis_index("col")
@@ -82,6 +82,8 @@
 
     own_copy = pltpu.make_async_copy(feat, fx.at[pl.ds(4, ROWS), pl.ds(0, COLS)], in_sem)
     own_copy.start()
+    gains_copy = pltpu.make_async_copy(gains_in, gains, g_sem)
+    gains_copy.start()
 
     def weights(l):
         for b in range(3):
@@ -162,6 +164,7 @@
         pk[1, at] = flat(value[:, COLS - 8 :])
         u0[pl.ds(row + 4, R), :COLS] = norm_act(value, gain(0), None)
 
+    gains_copy.wait()
     own_copy.wait()
     loop(4, own_act)
     pl.semaphore_wait(barrier, sum(jnp.where(there(dr, dc), 1, 0) for dr, dc in greet))
@@ -436,13 +439,14 @@
                 third_received(2 * turn)
                 third_received(2 * turn + 1)
 
+        @pl.when(g == 1)
+        def _():
+            far_send(0)
+            far_send(1)
+
         layer3_pair(g)
 
     loop(2, layer3_turn)
-    for k in (0, 1):
-        far_send(k)
-    for k in (0, 1):
-        far_sent(k)
     for k in (2, 3):
         far_send(k)
 
@@ -460,14 +464,11 @@
 
     loop(4, far_step)
 
-    def out_copy(k):
+    def far_end(k):
         row = row_of(k)
-        return pltpu.make_async_copy(s.at[pl.ds(row + 2, R), pl.ds(0, COLS)], out.at[pl.ds(row, R)], o_sem.at[k])
-
-    def far_end(k):
         move(k, False, "received", fp, fq, fp_s, fp_r)
-        add(row_of(k), fq[k, 0].astype(jnp.float32) + fq[k, 1].astype(jnp.float32))
-        out_copy(k).start()
+        far_sum = fq[k, 0].astype(jnp.float32) + fq[k, 1].astype(jnp.float32)
+        out[pl.ds(row, R)] = s[pl.ds(row + 2, R), :COLS] + far_sum
 
     loop(4, far_end)
 
@@ -481,12 +482,8 @@
             sent(*args)
 
     def all_sent(k):
-        @pl.when(k >= 2)
-        def _():
-            far_sent(k)
-
+        far_sent(k)
         move(k, False, "sent", fp, fq, fp_s, fp_r)
-        out_copy(k).wait()
 
     loop(4, all_sent)
 
@@ -494,13 +491,14 @@
 def local(nrow, ncol, features, inner_weights, far_weights, gains):
     bf16, f32 = jnp.bfloat16, jnp.float32
     dma = pltpu.SemaphoreType.DMA
-    hbm = pl.BlockSpec(memory_space=pl.ANY)
+    hbm = pl.BlockSpec(memory_space=pltpu.HBM)
     return pl.pallas_call(
         functools.partial(kernel, nrow, ncol),
         out_shape=jax.ShapeDtypeStruct(features.shape, f32),
-        in_specs=[hbm, hbm, hbm, pl.BlockSpec(memory_space=pltpu.VMEM)],
-        out_specs=hbm,
+        in_specs=[hbm] * 4,
+        out_specs=pl.BlockSpec(memory_space=pltpu.VMEM),
         scratch_shapes=[
+            pltpu.VMEM(gains.shape, f32),
             pltpu.VMEM((ROWS + 8, WIDE, CH), bf16),
             pltpu.VMEM((2, ROWS * 8, CH), bf16),
             pltpu.VMEM((2, (ROWS + 8) * 8, CH), bf16),
@@ -518,7 +516,7 @@
             pltpu.VMEM((4, 2, R, COLS, CH), bf16),
             pltpu.VMEM((4, 2, R, COLS, CH), bf16),
             pltpu.VMEM((4, 2, R, COLS, CH), bf16),
-            dma, dma((6,)), dma((4,)),
+            dma, dma, dma((6,)),
             dma((8,)), dma((8,)), dma((2,)), dma((2,)), dma((4,)), dma((4,)),
             dma((4, 2)), dma((4, 2)), dma((4, 2)), dma((4, 2)), dma((4, 2)), dma((4, 2)), dma((4, 2)), dma((4, 2)),
         ],

time: 68 us -> 66.9 us (0.984)
  no operation moved by 1% of the time
where the time goes in v2:
time: 66.9 us; the launch traced here: 66.7 us
  Pallas kernels  63.7 us (95%)
  local copies, waits for them, and re-layouts  2.98 us (4%)
    pallas_call x1, Pallas kernels, local(): pl.pallas_call(functools.partial(kernel, nrow, ncol), out_shape=jax.Shape...  63.7 us
    unnamed x5, local copies, waits for them, and re-layouts  2.98 us

profile of v2, /device:TPU:233, one launch (start us, length us, event | category | flops | bytes accessed | tf_op | source)
XLA Modules:
  0.0 66.7 jit_solution(11184528914114255721)
XLA Ops:
  0.0 0.0 copy-start
  0.0 1.1 %copy-done = bf16[16,64,384]{2,1,0:T(8,128)(2,1)S(1)} copy-done((bf16[16,64,384]{2,1,0:T(8,128)(2,1)S(1)}, bf16[16,64,384]{2,1,0:T(8,128)(2,1)}, u32[]{:S(2)}) %copy-start) | copy-done | bytes 786456
  1.1 0.0 copy-start.1
  1.1 0.7 %copy-done.1 = f32[5,384]{1,0:T(8,128)S(1)} copy-done((f32[5,384]{1,0:T(8,128)S(1)}, f32[5,384]{1,0:T(8,128)}, u32[]{:S(2)}) %copy-start.1) | copy-done | bytes 7704
  1.8 63.7 %shard_map.46 = f32[16,64,384]{2,1,0:T(8,128)S(1)} custom-call(bf16[16,64,384]{2,1,0:T(8,128)(2,1)S(1)} %copy-done, bf16[4,3,3,384,384]{4,3,2,1,0:T(8,128)(2,1)} %inner.1, bf16[3,3,384,384]{3,2,1,0:T(8,128)(2,1)} %far.1, f32[5,384]{1,0:T(8,128)S(1)} %copy-done.1), custom_call_target="tpu_custom_call" | custom-call | tf_op jit(solution)/shard_map/pallas_call | solution.py:495
  65.5 1.1 %copy.6 = f32[16,64,384]{2,1,0:T(8,128)} copy(f32[16,64,384]{2,1,0:T(8,128)S(1)} %shard_map.46) | data formatting | bytes 3145728
Async XLA Ops:
  0.0 1.1 %copy-start = (bf16[16,64,384]{2,1,0:T(8,128)(2,1)S(1)}, bf16[16,64,384]{2,1,0:T(8,128)(2,1)}, u32[]{:S(2)}) copy-start(bf16[16,64,384]{2,1,0:T(8,128)(2,1)} %feat.1) | copy-start | bytes 2359300
  1.1 0.7 %copy-start.1 = (f32[5,384]{1,0:T(8,128)S(1)}, f32[5,384]{1,0:T(8,128)}, u32[]{:S(2)}) copy-start(f32[5,384]{1,0:T(8,128)} %gains_in.1) | copy-start | bytes 23044

commit v3 on v2

--- a/solution.py
+++ b/solution.py
@@ -192,8 +192,9 @@
     for l in range(1, 4):
         weights(l)
     for t in range(3):
-        pltpu.make_async_copy(far.at[t], wf.at[0, :, :, pl.ds(t * CH, CH)], w_sem.at[4]).start()
-        pltpu.make_async_copy(far.at[:, t], wf.at[1, :, :, pl.ds(t * CH, CH)], w_sem.at[5]).start()
+        place = pl.ds((0, 2, 1)[t] * CH, CH)
+        pltpu.make_async_copy(far.at[t], wf.at[0, :, :, place], w_sem.at[4]).start()
+        pltpu.make_async_copy(far.at[:, t], wf.at[1, :, :, place], w_sem.at[5]).start()
 
     def weights_here(l):
         ref = w.at[l] if l < 4 else wf.at[l - 4]
@@ -324,19 +325,19 @@
             yield src, here, x3_s.at[k, side], x3_r.at[k, side], 0, dc
             yield src, corner, d3_s.at[k, side], d3_r.at[k, side], third[k][2], dc
 
-    def third_send(k):
-        src, dst, dr, dc = third[k]
-        send(src, dst, e3_s.at[k], e3_r.at[k], dr, dc)
-        for args in columns(k):
-            send(*args)
-
-    third_send(0)
-    third_send(1)
+    def third_send(*steps):
+        for k in steps:
+            src, dst, dr, dc = third[k]
+            send(src, dst, e3_s.at[k], e3_r.at[k], dr, dc)
+        for k in steps:
+            for args in columns(k):
+                send(*args)
+
+    third_send(0, 1)
     for k, (src, dst, dr, dc) in enumerate(second):
         received(dst, e2_s.at[k], e2_r.at[k], -dr, -dc)
     unrolled(2, lambda i: layer2(12 * i))
-    third_send(2)
-    third_send(3)
+    third_send(2, 3)
 
     def spread_cols(z):
         z = [z[:, b * CH : (b + 1) * CH].reshape(R, COLS, CH) for b in range(3)]
@@ -456,11 +457,12 @@
         left_side = jnp.concatenate(
             [v.reshape(R * COLS, CH) for v in (fr[k, 0], fa[k], fr[k, 1])], axis=-1
         )
-        z = dot(left_side, wf[lax.rem(k, 2)].reshape(3 * CH, 3 * CH))
+        weight = wf[lax.rem(k, 2)].reshape(3 * CH, 3 * CH)
+        z = dot(left_side, weight[:, : 2 * CH])
         fp[k, 0] = z[:, :CH].astype(jnp.bfloat16).reshape(R, COLS, CH)
-        fp[k, 1] = z[:, 2 * CH :].astype(jnp.bfloat16).reshape(R, COLS, CH)
+        fp[k, 1] = z[:, CH :].astype(jnp.bfloat16).reshape(R, COLS, CH)
         move(k, False, "send", fp, fq, fp_s, fp_r)
-        add(row, z[:, CH : 2 * CH].reshape(R, COLS, CH))
+        add(row, dot(left_side, weight[:, 2 * CH :]).reshape(R, COLS, CH))
 
     loop(4, far_step)
 

time: 66.9 us -> 66.6 us (level)
  no operation moved by 1% of the time
where the time goes in v3:
time: 66.6 us; the launch traced here: 66.4 us
  Pallas kernels  63.4 us (95%)
  local copies, waits for them, and re-layouts  2.98 us (4%)
    pallas_call x1, Pallas kernels, local(): pl.pallas_call(functools.partial(kernel, nrow, ncol), out_shape=jax.Shape...  63.4 us
    unnamed x5, local copies, waits for them, and re-layouts  2.98 us

profile of v3, /device:TPU:233, one launch (start us, length us, event | category | flops | bytes accessed | tf_op | source)
XLA Modules:
  0.0 66.4 jit_solution(10029220485792272640)
XLA Ops:
  0.0 0.0 copy-start
  0.0 1.1 %copy-done = bf16[16,64,384]{2,1,0:T(8,128)(2,1)S(1)} copy-done((bf16[16,64,384]{2,1,0:T(8,128)(2,1)S(1)}, bf16[16,64,384]{2,1,0:T(8,128)(2,1)}, u32[]{:S(2)}) %copy-start) | copy-done | bytes 786456
  1.1 0.0 copy-start.1
  1.1 0.7 %copy-done.1 = f32[5,384]{1,0:T(8,128)S(1)} copy-done((f32[5,384]{1,0:T(8,128)S(1)}, f32[5,384]{1,0:T(8,128)}, u32[]{:S(2)}) %copy-start.1) | copy-done | bytes 7704
  1.8 63.4 %shard_map.46 = f32[16,64,384]{2,1,0:T(8,128)S(1)} custom-call(bf16[16,64,384]{2,1,0:T(8,128)(2,1)S(1)} %copy-done, bf16[4,3,3,384,384]{4,3,2,1,0:T(8,128)(2,1)} %inner.1, bf16[3,3,384,384]{3,2,1,0:T(8,128)(2,1)} %far.1, f32[5,384]{1,0:T(8,128)S(1)} %copy-done.1), custom_call_target="tpu_custom_call" | custom-call | tf_op jit(solution)/shard_map/pallas_call | solution.py:497
  65.3 1.1 %copy.6 = f32[16,64,384]{2,1,0:T(8,128)} copy(f32[16,64,384]{2,1,0:T(8,128)S(1)} %shard_map.46) | data formatting | bytes 3145728
Async XLA Ops:
  0.0 1.1 %copy-start = (bf16[16,64,384]{2,1,0:T(8,128)(2,1)S(1)}, bf16[16,64,384]{2,1,0:T(8,128)(2,1)}, u32[]{:S(2)}) copy-start(bf16[16,64,384]{2,1,0:T(8,128)(2,1)} %feat.1) | copy-start | bytes 2359300
  1.1 0.7 %copy-start.1 = (f32[5,384]{1,0:T(8,128)S(1)}, f32[5,384]{1,0:T(8,128)}, u32[]{:S(2)}) copy-start(f32[5,384]{1,0:T(8,128)} %gains_in.1) | copy-start | bytes 23044

commit v4 on v3

--- a/solution.py
+++ b/solution.py
@@ -287,12 +287,12 @@
         pk3[1, at] = flat(act[:, COLS - 8 :])
 
     weights_here(0)
-    loop(3, lambda i: layer0_own(2 + R * i))
+    unrolled(3, lambda i: layer0_own(2 + R * i))
     first_received(6)
     first_received(7)
     loop(4, halo_act)
     layer0_halo_dot()
-    loop(3, layer0_halo)
+    unrolled(3, layer0_halo)
     for k in range(6):
         first_received(k)
     loop(2, outer_act)

time: 66.6 us -> 74.6 us (1.12)
  the two profiles are of different devices: /device:TPU:233 before, /device:TPU:109 now
where the time goes in v4:
time: 74.6 us; the launch traced here: 74.4 us
  Pallas kernels  71.4 us (96%)
  local copies, waits for them, and re-layouts  2.98 us (4%)
    pallas_call x1, Pallas kernels, local(): pl.pallas_call(functools.partial(kernel, nrow, ncol), out_shape=jax.Shape...  71.4 us
    unnamed x5, local copies, waits for them, and re-layouts  2.98 us

profile of v4, /device:TPU:109, one launch (start us, length us, event | category | flops | bytes accessed | tf_op | source)
XLA Modules:
  0.0 74.4 jit_solution(2987775003612191563)
XLA Ops:
  0.0 0.0 copy-start
  0.0 1.1 %copy-done = bf16[16,64,384]{2,1,0:T(8,128)(2,1)S(1)} copy-done((bf16[16,64,384]{2,1,0:T(8,128)(2,1)S(1)}, bf16[16,64,384]{2,1,0:T(8,128)(2,1)}, u32[]{:S(2)}) %copy-start) | copy-done | bytes 786456
  1.1 0.0 copy-start.1
  1.1 0.7 copy-done.1
  1.8 71.4 %shard_map.46 = f32[16,64,384]{2,1,0:T(8,128)S(1)} custom-call(bf16[16,64,384]{2,1,0:T(8,128)(2,1)S(1)} %copy-done, bf16[4,3,3,384,384]{4,3,2,1,0:T(8,128)(2,1)} %inner.1, bf16[3,3,384,384]{3,2,1,0:T(8,128)(2,1)} %far.1, f32[5,384]{1,0:T(8,128)S(1)} %copy-done.1), custom_call_target="tpu_custom_call" | custom-call | tf_op jit(solution)/shard_map/pallas_call | solution.py:497
  73.3 1.1 %copy.6 = f32[16,64,384]{2,1,0:T(8,128)} copy(f32[16,64,384]{2,1,0:T(8,128)S(1)} %shard_map.46) | data formatting | bytes 3145728
Async XLA Ops:
  0.0 1.1 %copy-start = (bf16[16,64,384]{2,1,0:T(8,128)(2,1)S(1)}, bf16[16,64,384]{2,1,0:T(8,128)(2,1)}, u32[]{:S(2)}) copy-start(bf16[16,64,384]{2,1,0:T(8,128)(2,1)} %feat.1) | copy-start | bytes 2359300
  1.1 0.7 copy-start.1
